TPU v7x, 512 devices: a whole 4x8x8 slice. The times are simulated.
512 devices in a mesh: frames: 64 (over x, y, core), heads: 8 (over z).
Axes of the slice: x: 4, y: 8, z: 8, core: 2. Of those that a mesh axis runs over, the one named last changes fastest.
Arguments:
- query_states: bfloat16 [98304, 1024], P('frames', 'heads'), may hold values from -9 to 9
- key_states: bfloat16 [98304, 1024], P('frames', 'heads'), may hold values from -9 to 9
- value_states: bfloat16 [98304, 1024], P('frames', 'heads'), may hold values from -6 to 6
- pair_list: int32 [4096, 2], replicated, may hold values from 0 to 511, as said below
- out_weight: bfloat16 [1024, 1024], P('heads'), may hold values from -0.1875 to 0.1875
Outputs:
- attended: bfloat16 [98304, 1024], P('frames', 'heads')
Inputs may be any that keep to these rules, and one draw needn't show every extreme that they name: `pair_list`: row r belongs to device r // 64 of frames: its first frame is held by that device (frames f * 8 to f * 8 + 7 on device f), its second frame j lies on device j // 8. Among the 64 rows of one device at most 1 have their second frame on any one device, and some device is reached exactly 1 times. The two frames of a row differ.
All inputs are finite; a program needn't handle non-finite values.
Results may differ from a plain program's by a relative error of at most 0.017.
Values may be sent and summed in bfloat16 or wider, within the bound.
A program may use at most 128 MiB of HBM per device.

v0:
```python
import jax
import jax.numpy as jnp
from jax import lax
from jax.experimental import pallas as pl
from jax.experimental.pallas import tpu as pltpu
from jax.sharding import PartitionSpec as P

MESH = pl.DeviceIdType.MESH
BF = jnp.bfloat16
F32 = jnp.float32
TOKF, HDIM = 192, 64
X, Y, Z = 4, 8, 8
FR = 8
ROWS = FR * TOKF
RA = 80
WHOLE = (0, FR, 0, TOKF)
A_PART = (0, FR, 0, RA)
B_PART = (0, FR, RA, TOKF - RA)
A_HALF = {1: (0, FR // 2, 0, RA), -1: (FR // 2, FR // 2, 0, RA)}
B_HALF = {1: (0, FR // 2, RA, TOKF - RA), -1: (FR // 2, FR // 2, RA, TOKF - RA)}
UNITS = 136
PER = 8
LOOPS = UNITS // PER
DIRS = (1, -1)
ORDER = (0, -1, 1, -2, 2, -3, 3, 4)


def tables(pair_list, me):
    first = pair_list[:, 0].reshape(64, 64)
    second = pair_list[:, 1].reshape(64, 64)
    own_first = lax.dynamic_index_in_dim(first, me, 0, keepdims=False) - me * FR
    own_second = lax.dynamic_index_in_dim(second, me, 0, keepdims=False)
    mine = second // FR == me
    back_frame = jnp.sum(jnp.where(mine, second, 0), axis=1) - me * FR
    back_other = jnp.sum(jnp.where(mine, first, 0), axis=1)
    here = jnp.arange(FR, dtype=jnp.int32)
    frame = jnp.concatenate([here, own_first, back_frame])
    other = jnp.concatenate([here + me * FR, own_second, back_other])
    number = jnp.arange(UNITS, dtype=jnp.int32)
    ahead = (frame[None, :] < frame[:, None]) | (
        (frame[None, :] == frame[:, None]) & (number[None, :] < number[:, None])
    )
    place = jnp.sum(ahead.astype(jnp.int32), axis=1)
    hit = place[None, :] == number[:, None]
    frame_at = jnp.sum(jnp.where(hit, frame[None, :], 0), axis=1)
    other_at = jnp.sum(jnp.where(hit, other[None, :], 0), axis=1)
    same = jnp.sum(jnp.where(hit, (number >= FR).astype(jnp.int32)[None, :], 0), axis=1)
    last = jnp.sum((frame[None, :] <= number[:, None]).astype(jnp.int32), axis=1) - 1
    last = jnp.maximum(jnp.minimum(last, UNITS - 1), 0)
    source = other_at // FR
    fresh = jnp.where(same > 0, 0.0, -jnp.inf).astype(F32)
    return fresh[None, :], jnp.stack(
        [
            source % 2,
            source // (2 * Y),
            (source // 2) % Y,
            other_at % FR,
            frame_at,
            last,
        ]
    )


def kernel(
    tab, fresh, q_ref, k_ref, v_ref, w_ref, o_ref,
    buf0, buf1, slots, qz, mz0, mz1, wbuf, total, high, acc,
    send_sem, near_send, near_recv, recv_sem, w_send, w_recv, z_send, z_recv,
):
    bufs, mzs = (buf0, buf1), (mz0, mz1)
    me = lax.axis_index("frames")
    z = lax.axis_index("heads")
    x, y, c = me // (2 * Y), (me // 2) % Y, me % 2

    def ring(value, size):
        return lax.rem(value + 4 * size, size)

    def at(dx, dy):
        return (ring(x + dx, X) * (2 * Y) + ring(y + dy, Y) * 2 + c, z)

    partner = (x * (2 * Y) + y * 2 + (1 - c), z)

    def zat(dz):
        return (me, ring(z + dz, Z))

    barrier = pltpu.get_barrier_semaphore()
    peers = [at(1, 0), at(-1, 0), at(0, 1), at(0, -1), partner] + [zat(d) for d in range(1, Z)]
    for peer in peers:
        pl.semaphore_signal(barrier, inc=1, device_id=peer, device_id_type=MESH)

    lane = lax.broadcasted_iota(jnp.int32, (TOKF, 128), 1)
    low = lane < HDIM

    def prepare(head):
        for f in range(FR):
            rows = pl.ds(f * TOKF, TOKF)
            turned = pltpu.roll(v_ref[rows, :], HDIM, 1)
            keyed = k_ref[rows, :]
            block = jnp.where(low, keyed, turned) if head == 0 else jnp.where(low, turned, keyed)
            bufs[head][c, x, y, f] = block
            query = q_ref[rows, :] * jnp.asarray(0.125, BF)
            nil = jnp.zeros_like(query)
            qz[head, f] = jnp.where(low, query, nil) if head == 0 else jnp.where(low, nil, query)

    prepare(0)
    pl.semaphore_wait(barrier, len(peers))

    names = {}

    def sem_of(name):
        return names.setdefault(name, len(names))

    sent = {}
    near_sent = {}
    def view(head, spec):
        dx, dy, part = spec
        by = ring(y + dy, Y)
        frames, rows = pl.ds(part[0], part[1]), pl.ds(part[2], part[3])
        if dx is None:
            return bufs[head].at[c, :, by, frames, rows, :]
        return bufs[head].at[c, ring(x + dx, X), by, frames, rows, :]

    def link_copy(head, name, spec, device):
        number = sem_of(name)
        ref = view(head, spec)
        return pltpu.make_async_remote_copy(
            src_ref=ref, dst_ref=ref, send_sem=send_sem.at[number], recv_sem=recv_sem.at[head, number],
            device_id=device, device_id_type=MESH,
        )

    def near_copy(head, name, spec):
        number = near_names.setdefault(name, len(near_names))
        ref = view(head, spec)
        return pltpu.make_async_remote_copy(
            src_ref=ref, dst_ref=ref, send_sem=near_send.at[number], recv_sem=near_recv.at[head],
            device_id=partner, device_id_type=MESH,
        )

    def remote(head, name, spec, hop):
        if head == 1:
            link_copy(0, name, spec, partner).wait_send()
        link_copy(head, name, spec, at(*hop)).start()
        sent[name] = spec

    def arrive(head, name, spec):
        link_copy(head, name, spec, partner).wait_recv()

    def near(head, name, spec):
        if head == 1:
            near_copy(0, name, spec).wait_send()
        near_copy(head, name, spec).start()
        near_sent[name] = spec

    near_names = {}

    def start_x(head, k):
        for d in DIRS:
            remote(head, ("x1", k, d), (0, k, B_PART), (d, 0))

    def start_own(head):
        near(head, "own", (0, 0, WHOLE))
        for d in DIRS:
            remote(head, ("a1", d), (0, 0, A_PART), (d, 0))
        for d in DIRS:
            remote(head, ("b", 1, d), (0, 0, B_PART), (0, d))
        start_x(head, 0)

    def on_a1(head):
        for d in DIRS:
            arrive(head, ("a1", d), (-d, 0, A_PART))
            remote(head, ("a2", d), (-d, 0, A_HALF[d]), (d, 0))
            near(head, ("a1", d), (-d, 0, A_PART))

    def on_a2(head):
        for d in DIRS:
            arrive(head, ("a2", d), (2, 0, A_HALF[d]))
        for d in DIRS:
            remote(head, ("y", 1, d), (None, 0, A_PART), (0, d))
        near(head, "a2", (2, 0, A_PART))

    def on_b(head, k):
        if k < 4:
            for d in DIRS:
                arrive(head, ("b", k, d), (0, -d * k, B_PART))
                part = B_PART if k < 3 else B_HALF[d]
                remote(head, ("b", k + 1, d), (0, -d * k, part), (0, d))
                start_x(head, -d * k)
                near(head, ("b", k, d), (0, -d * k, B_PART))
        else:
            for d in DIRS:
                arrive(head, ("b", 4, d), (0, 4, B_HALF[d]))
            start_x(head, 4)
            near(head, ("b", 4), (0, 4, B_PART))

    def on_x1(head, k):
        for d in DIRS:
            arrive(head, ("x1", k, d), (-d, k, B_PART))
            remote(head, ("x2", k, d), (-d, k, B_HALF[d]), (d, 0))
            near(head, ("x1", k, d), (-d, k, B_PART))

    def on_x2(head, k):
        for d in DIRS:
            arrive(head, ("x2", k, d), (2, k, B_HALF[d]))
        near(head, ("x2", k), (2, k, B_PART))

    def on_y(head, k):
        if k < 4:
            for d in DIRS:
                arrive(head, ("y", k, d), (None, -d * k, A_PART))
                part = A_PART if k < 3 else A_HALF[d]
                remote(head, ("y", k + 1, d), (None, -d * k, part), (0, d))
                near(head, ("y", k, d), (None, -d * k, A_PART))
        else:
            for d in DIRS:
                arrive(head, ("y", 4, d), (None, 4, A_HALF[d]))
            near(head, ("y", 4), (None, 4, A_PART))

    def near_done(head):
        ref = bufs[head].at[1 - c]
        pltpu.make_async_remote_copy(
            src_ref=ref, dst_ref=ref, send_sem=near_send.at[0], recv_sem=near_recv.at[head],
            device_id=partner, device_id_type=MESH,
        ).wait_recv()

    def events(head):
        first = [lambda: on_a1(head), lambda: on_b(head, 1), lambda: on_a2(head)]
        first += [lambda k=k: on_b(head, k) for k in (2, 3, 4)]
        rest = []
        for i, k in enumerate(ORDER):
            rest.append(lambda k=k: on_x1(head, k))
            rest.append(lambda k=k: on_x2(head, k))
            if i % 2 == 1:
                rest.append(lambda k=i // 2 + 1: on_y(head, k))
        return first, rest

    def compute(head, iteration):
        buf = bufs[head]
        ones_at = low if head == 0 else jnp.logical_not(low)
        one, out = (0, HDIM) if head == 0 else (HDIM, 0)
        m, a = high[...], acc[...]
        for u in range(PER):
            t = iteration * PER + u
            kv = buf[tab[0, t], tab[1, t], tab[2, t], tab[3, t]]
            query = qz[head, tab[4, t]]
            s = lax.dot_general(kv, query, (((1,), (1,)), ((), ())), preferred_element_type=F32)
            m_prev = m + fresh[0, t]
            m = jnp.maximum(m_prev, jnp.max(s, axis=0, keepdims=True))
            p = jnp.exp(s - m).astype(BF)
            alpha = jnp.exp(m_prev - m)
            side = jnp.where(ones_at, jnp.ones_like(kv), kv)
            a = a * alpha + lax.dot_general(
                side, p, (((0,), (0,)), ((), ())), preferred_element_type=F32
            )
            slots[t] = (a[out : out + HDIM] / a[one : one + HDIM]).astype(BF)
        high[...] = m
        acc[...] = a

    def gather_merged(head):
        for f in range(FR // 2):
            both = jnp.concatenate([slots[tab[5, f]], slots[tab[5, f + FR // 2]]], axis=0)
            mzs[head][z, pl.ds(f * TOKF, TOKF), :] = both.T

    zrows = FR // 2 * TOKF
    z_half = {1: (0, zrows // 2), -1: (zrows // 2, zrows // 2)}

    def z_copy(head, k, d, source, part, device):
        ref = mzs[head].at[source, pl.ds(part[0], part[1]), :]
        number = 2 * (k - 1) + (d < 0)
        return pltpu.make_async_remote_copy(
            src_ref=ref, dst_ref=ref, send_sem=z_send.at[head, number], recv_sem=z_recv.at[head, number],
            device_id=device, device_id_type=MESH,
        )

    z_sent = []

    def z_start(head, k, d, source, part):
        copy = z_copy(head, k, d, source, part, zat(d))
        copy.start()
        z_sent.append(copy)

    def z_first(head):
        for d in DIRS:
            z_start(head, 1, d, z, (0, zrows))

    def on_z(head, k):
        sources = []
        for d in DIRS:
            source = ring(z - d * k, Z)
            z_copy(head, k, d, source, z_half[d] if k == 4 else (0, zrows), partner).wait_recv()
            if k < 4:
                z_start(head, k + 1, d, source, z_half[d] if k == 3 else (0, zrows))
                sources.append(source)
            elif d < 0:
                sources.append(source)
        for source in sources:
            project(head, source)

    def project(head, source, begin=False):
        w = wbuf[source, pl.ds(head * HDIM, HDIM), :]
        nil = jnp.zeros_like(w)
        wide = jnp.concatenate(
            [jnp.concatenate([w, nil], axis=1), jnp.concatenate([nil, w], axis=1)], axis=0
        )
        term = jnp.dot(mzs[head][source], wide, preferred_element_type=F32)
        total[...] = term if begin else total[...] + term

    w_copies = []
    for d in range(1, Z):
        target = ring(z + d, Z)
        start = pl.multiple_of(target * 128, 128)
        copy = pltpu.make_async_remote_copy(
            src_ref=w_ref.at[:, pl.ds(start, 128)], dst_ref=wbuf.at[z],
            send_sem=w_send.at[d - 1], recv_sem=w_recv.at[d - 1],
            device_id=zat(d), device_id_type=MESH,
        )

        w_copies.append(copy)

    start_own(0)
    for copy in w_copies:
        copy.start()
    prepare(1)
    wbuf[z] = w_ref[:, pl.ds(pl.multiple_of(z * 128, 128), 128)]
    high[...] = jnp.zeros_like(high)
    acc[...] = jnp.zeros_like(acc)

    first, rest = events(0)
    for event in first + rest[:-3]:
        event()
    start_own(1)
    for event in rest[-3:]:
        event()
    near_done(0)
    first, rest = events(1)
    for event in first:
        event()
    ahead = LOOPS

    @pl.loop(0, LOOPS)
    def _(iteration):
        for number, event in enumerate(rest[:ahead]):
            pl.when(iteration == number)(event)
        compute(0, iteration)

    rest = rest[ahead:]
    gather_merged(0)
    z_first(0)
    for copy in w_copies:
        copy.wait_recv()
    project(0, z, begin=True)
    steps = [lambda k=k: on_z(0, k) for k in (1, 2, 3, 4)]
    while rest or steps:
        if rest:
            rest.pop(0)()
        if steps:
            steps.pop(0)()
    near_done(1)

    @pl.loop(0, LOOPS)
    def _(iteration):
        compute(1, iteration)

    gather_merged(1)
    z_first(1)
    project(1, z)
    for k in (1, 2, 3, 4):
        on_z(1, k)
    for f in range(FR):
        half = f // (FR // 2)
        rows = (f % (FR // 2)) * TOKF
        o_ref[pl.ds(f * TOKF, TOKF), :] = total[
            pl.ds(rows, TOKF), pl.ds(half * 128, 128)
        ].astype(BF)
    for name, spec in sent.items():
        link_copy(1, name, spec, partner).wait_send()
    for name, spec in near_sent.items():
        near_copy(1, name, spec).wait_send()
    for copy in z_sent + w_copies:
        copy.wait_send()


def body(query_states, key_states, value_states, pair_list, out_weight):
    me = lax.axis_index("frames")
    fresh, tab = tables(pair_list, me)
    vmem = pl.BlockSpec(memory_space=pltpu.VMEM)
    smem = pl.BlockSpec(memory_space=pltpu.SMEM)
    return pl.pallas_call(
        kernel,
        out_shape=jax.ShapeDtypeStruct((ROWS, 128), BF),
        in_specs=[smem, smem, vmem, vmem, vmem, vmem],
        out_specs=vmem,
        scratch_shapes=[
            pltpu.VMEM((2, X, Y, FR, TOKF, 128), BF),
            pltpu.VMEM((2, X, Y, FR, TOKF, 128), BF),
            pltpu.VMEM((UNITS, HDIM, TOKF), BF),
            pltpu.VMEM((2, FR, TOKF, 128), BF),
            pltpu.VMEM((Z, FR // 2 * TOKF, 128), BF),
            pltpu.VMEM((Z, FR // 2 * TOKF, 128), BF),
            pltpu.VMEM((Z, 128, 128), BF),
            pltpu.VMEM((FR // 2 * TOKF, 256), F32),
            pltpu.VMEM((1, TOKF), F32),
            pltpu.VMEM((128, TOKF), F32),
            pltpu.SemaphoreType.DMA((52,)),
            pltpu.SemaphoreType.DMA((42,)),
            pltpu.SemaphoreType.DMA((2,)),
            pltpu.SemaphoreType.DMA((2, 52)),
            pltpu.SemaphoreType.DMA((7,)),
            pltpu.SemaphoreType.DMA((7,)),
            pltpu.SemaphoreType.DMA((2, 8)),
            pltpu.SemaphoreType.DMA((2, 8)),
        ],
        compiler_params=pltpu.CompilerParams(
            collective_id=0, has_side_effects=True, vmem_limit_bytes=63 * 2**20
        ),
        name="scene_attention",
    )(tab, fresh, query_states, key_states, value_states, out_weight)


def solution(mesh):
    placed = (
        P("frames", "heads"),
        P("frames", "heads"),
        P("frames", "heads"),
        P(),
        P("heads", None),
    )
    return jax.shard_map(
        body, mesh=mesh, in_specs=placed, out_specs=P("frames", "heads"), check_vma=False
    )
```

profile of v0, /device:TPU:80, one launch (start us, length us, event | category | flops | bytes accessed | tf_op | source)
XLA Modules:
  0.0 282.6 jit_solution(2619604801243637292)
XLA Ops:
  0.0 0.9 slice_reduce_fusion
  0.9 0.1 reshape_squeeze.7
  1.0 0.1 reshape_squeeze.6
  1.1 0.1 select_reduce_fusion.4
  1.2 0.1 pad_add_fusion
  1.3 0.1 pad_add_fusion.1
  1.4 0.2 convert_reduce_fusion.1
  1.6 0.2 select_reduce_fusion
  1.8 0.6 compare_select_fusion.5
  2.5 0.6 stack.5.tab
  3.1 277.8 %scene_attention.1 = bf16[1536,128]{1,0:T(8,128)(2,1)} custom-call(s32[6,136]{1,0:T(8,128)} %stack.5.tab, f32[1,136]{1,0:T(1,128)} %bitcast.10, bf16[1536,128]{1,0:T(8,128)(2,1)} %q_ref.1, bf16[1536,128]{1,0:T(8,128)(2,1)} %k_ref.1, bf16[1536,128]{1,0:T(8,128)(2,1)} %v_ref.1, bf16[128,1024]{1,0:T(8,128)(2,1)} %w_ref.1), custom_call_target="tpu_custom_call" | custom-call | tf_op jit(solution)/shard_map/scene_attention/pallas_call | solution.py:386
  280.9 1.8 copy.7
  (10 shorter events, 0.1 us)
where the time goes:
time: 283 us
  Pallas kernels  278 us (98%)
  local copies, waits for them, and re-layouts  3.45 us (1%)
    pallas_call x1, Pallas kernels, body(): pl.pallas_call(kernel, out_shape=jax.ShapeDtypeStruct((ROWS, 128), BF), i...  278 us

commit v1 on v0

v1 whole, which is shorter than its diff:
```python
import jax
import jax.numpy as jnp
from jax import lax
from jax.experimental import pallas as pl
from jax.experimental.pallas import tpu as pltpu
from jax.sharding import PartitionSpec as P

MESH = pl.DeviceIdType.MESH
BF = jnp.bfloat16
F32 = jnp.float32
TOKF, HDIM = 192, 64
X, Y, Z = 4, 8, 8
FR = 8
ROWS = FR * TOKF
RA = 80
WHOLE = (0, FR, 0, TOKF)
A_PART = (0, FR, 0, RA)
B_PART = (0, FR, RA, TOKF - RA)
A_HALF = {1: (0, FR // 2, 0, RA), -1: (FR // 2, FR // 2, 0, RA)}
B_HALF = {1: (0, FR // 2, RA, TOKF - RA), -1: (FR // 2, FR // 2, RA, TOKF - RA)}
UNITS = 136
PER = (8, 17)
DIRS = (1, -1)
AHEAD = (
    (0, ("a", 1)),
    (0, ("b", 1)),
    (0, ("w", 1)),
    (0, ("x", 0, 1)),
    (0, ("y", 0, 1)),
    (0, ("a", 2)),
    (0, ("w", 2)),
    (0, ("y", 1, 1)),
    (0, ("x", 1, 1)),
    (0, ("b", 2)),
    (0, ("w", 3)),
    (0, ("x", 0, 2)),
    (0, ("y", 0, 2)),
    (0, ("w", 4)),
    (0, ("y", 2, 1)),
    (0, ("x", 1, 2)),
    (0, ("y", 1, 2)),
    (0, ("x", 2, 1)),
    (0, ("b", 3)),
    (1, ("own", "y")),
    (0, ("y", 0, 3)),
    (0, ("x", 2, 2)),
    (0, ("y", 2, 2)),
    (0, ("y", 1, 3)),
    (0, ("x", 3, 1)),
    (1, ("own", "x")),
    (0, ("b", 4)),
    (1, ("b", 1)),
    (0, ("x", 3, 2)),
    (1, ("y", 0, 1)),
    (1, ("a", 1)),
    (0, ("y", 0, 4)),
    (0, ("y", 2, 3)),
    (1, ("x", 0, 1)),
    (0, ("y", 1, 4)),
    (0, ("x", 4, 1)),
    (1, ("b", 2)),
    (1, ("y", 0, 2)),
    (1, ("x", 1, 1)),
    (1, ("a", 2)),
    (1, ("y", 1, 1)),
    (1, ("x", 0, 2)),
    (0, ("y", 2, 4)),
    (0, ("x", 4, 2)),
)
BESIDE = (
    (2, (1, ("b", 3))),
    (6, (1, ("y", 0, 3))),
    (8, (1, ("x", 2, 1))),
    (8, (1, ("y", 2, 1))),
    (13, (1, ("x", 1, 2))),
    (15, (1, ("y", 1, 2))),
)
AFTER = (
    (1, ("b", 4)),
    (0, ("merge",)),
    (1, ("y", 0, 4)),
    (1, ("x", 3, 1)),
    (1, ("y", 2, 2)),
    (0, ("z", 1)),
    (1, ("x", 2, 2)),
    (1, ("y", 1, 3)),
    (1, ("x", 4, 1)),
    (1, ("y", 2, 3)),
    (0, ("z", 2)),
    (1, ("x", 3, 2)),
    (1, ("y", 1, 4)),
    (1, ("y", 2, 4)),
    (1, ("x", 4, 2)),
    (0, ("z", 3)),
    (0, ("z", 4)),
)


def tables(pair_list, me):
    first = pair_list[:, 0].reshape(64, 64)
    second = pair_list[:, 1].reshape(64, 64)
    own_first = lax.dynamic_index_in_dim(first, me, 0, keepdims=False) - me * FR
    own_second = lax.dynamic_index_in_dim(second, me, 0, keepdims=False)
    mine = second // FR == me
    back_frame = jnp.sum(jnp.where(mine, second, 0), axis=1) - me * FR
    back_other = jnp.sum(jnp.where(mine, first, 0), axis=1)
    here = jnp.arange(FR, dtype=jnp.int32)
    frame = jnp.concatenate([here, own_first, back_frame])
    other = jnp.concatenate([here + me * FR, own_second, back_other])
    number = jnp.arange(UNITS, dtype=jnp.int32)
    ahead = (frame[None, :] < frame[:, None]) | (
        (frame[None, :] == frame[:, None]) & (number[None, :] < number[:, None])
    )
    place = jnp.sum(ahead.astype(jnp.int32), axis=1)
    hit = place[None, :] == number[:, None]
    frame_at = jnp.sum(jnp.where(hit, frame[None, :], 0), axis=1)
    other_at = jnp.sum(jnp.where(hit, other[None, :], 0), axis=1)
    same = jnp.sum(jnp.where(hit, (number >= FR).astype(jnp.int32)[None, :], 0), axis=1)
    last = jnp.sum((frame[None, :] <= number[:, None]).astype(jnp.int32), axis=1) - 1
    last = jnp.maximum(jnp.minimum(last, UNITS - 1), 0)
    source = other_at // FR
    fresh = jnp.where(same > 0, 0.0, -jnp.inf).astype(F32)
    return fresh[None, :], jnp.stack(
        [
            source % 2,
            source // (2 * Y),
            (source // 2) % Y,
            other_at % FR,
            frame_at,
            last,
        ]
    )


def kernel(
    tab, fresh, q_ref, k_ref, v_ref, w_ref, o_ref,
    buf0, buf1, slots, qz, mz0, mz1, wbuf, total, high, acc,
    send_sem, near_send, near_recv, recv_sem, w_send, w_recv, z_send, z_recv,
):
    bufs, mzs = (buf0, buf1), (mz0, mz1)
    me = lax.axis_index("frames")
    z = lax.axis_index("heads")
    x, y, c = me // (2 * Y), (me // 2) % Y, me % 2

    def ring(value, size):
        return lax.rem(value + 4 * size, size)

    def at(dx, dy):
        return (ring(x + dx, X) * (2 * Y) + ring(y + dy, Y) * 2 + c, z)

    partner = (x * (2 * Y) + y * 2 + (1 - c), z)

    def zat(dz):
        return (me, ring(z + dz, Z))

    barrier = pltpu.get_barrier_semaphore()
    peers = [at(1, 0), at(-1, 0), at(0, 1), at(0, -1), partner] + [zat(1), zat(-1)]
    for peer in peers:
        pl.semaphore_signal(barrier, inc=1, device_id=peer, device_id_type=MESH)

    lane = lax.broadcasted_iota(jnp.int32, (TOKF, 128), 1)
    low = lane < HDIM

    def prepare(head):
        for f in range(FR):
            rows = pl.ds(f * TOKF, TOKF)
            turned = pltpu.roll(v_ref[rows, :], HDIM, 1)
            keyed = k_ref[rows, :]
            block = jnp.where(low, keyed, turned) if head == 0 else jnp.where(low, turned, keyed)
            bufs[head][c, x, y, f] = block
            query = q_ref[rows, :] * jnp.asarray(0.125, BF)
            nil = jnp.zeros_like(query)
            qz[head, f] = jnp.where(low, query, nil) if head == 0 else jnp.where(low, nil, query)

    prepare(0)
    pl.semaphore_wait(barrier, len(peers))

    names = {}

    def sem_of(name):
        return names.setdefault(name, len(names))

    sent = {}
    near_sent = {}
    def view(head, spec):
        dx, dy, part = spec
        by = ring(y + dy, Y)
        frames, rows = pl.ds(part[0], part[1]), pl.ds(part[2], part[3])
        if dx is None:
            return bufs[head].at[c, :, by, frames, rows, :]
        return bufs[head].at[c, ring(x + dx, X), by, frames, rows, :]

    def link_copy(head, name, spec, device):
        number = sem_of(name)
        ref = view(head, spec)
        return pltpu.make_async_remote_copy(
            src_ref=ref, dst_ref=ref, send_sem=send_sem.at[number], recv_sem=recv_sem.at[head, number],
            device_id=device, device_id_type=MESH,
        )

    def near_copy(head, name, spec):
        number = near_names.setdefault(name, len(near_names))
        ref = view(head, spec)
        return pltpu.make_async_remote_copy(
            src_ref=ref, dst_ref=ref, send_sem=near_send.at[number], recv_sem=near_recv.at[head],
            device_id=partner, device_id_type=MESH,
        )

    def remote(head, name, spec, hop):
        if head == 1:
            link_copy(0, name, spec, partner).wait_send()
        link_copy(head, name, spec, at(*hop)).start()
        sent[name] = spec

    def arrive(head, name, spec):
        link_copy(head, name, spec, partner).wait_recv()

    def near(head, name, spec):
        if head == 1:
            near_copy(0, name, spec).wait_send()
        near_copy(head, name, spec).start()
        near_sent[name] = spec

    near_names = {}

    def start_x(head, k):
        for d in DIRS:
            remote(head, ("x", k, 1, d), (0, k, B_PART), (d, 0))

    def start_y(head, j):
        for d in DIRS:
            remote(head, ("y", j, 1, d), (j, 0, A_PART), (0, d))

    def own_x(head):
        near(head, "own", (0, 0, WHOLE))
        for d in DIRS:
            remote(head, ("a", 1, d), (0, 0, A_PART), (d, 0))
        start_x(head, 0)

    def own_y(head):
        for d in DIRS:
            remote(head, ("b", 1, d), (0, 0, B_PART), (0, d))
        start_y(head, 0)

    def on_a(head, step):
        if step == 1:
            for d in DIRS:
                arrive(head, ("a", 1, d), (-d, 0, A_PART))
                remote(head, ("a", 2, d), (-d, 0, A_HALF[d]), (d, 0))
                start_y(head, -d)
                near(head, ("a", d), (-d, 0, A_PART))
        else:
            for d in DIRS:
                arrive(head, ("a", 2, d), (2, 0, A_HALF[d]))
            start_y(head, 2)
            near(head, "a", (2, 0, A_PART))

    def on_b(head, k):
        if k < 4:
            for d in DIRS:
                arrive(head, ("b", k, d), (0, -d * k, B_PART))
                part = B_PART if k < 3 else B_HALF[d]
                remote(head, ("b", k + 1, d), (0, -d * k, part), (0, d))
                start_x(head, -d * k)
                near(head, ("b", k, d), (0, -d * k, B_PART))
        else:
            for d in DIRS:
                arrive(head, ("b", 4, d), (0, 4, B_HALF[d]))
            start_x(head, 4)
            near(head, ("b", 4), (0, 4, B_PART))

    def on_x(head, distance, step):
        for k in sorted({-distance, distance}) if distance < 4 else [4]:
            for d in DIRS:
                if step == 1:
                    arrive(head, ("x", k, 1, d), (-d, k, B_PART))
                    remote(head, ("x", k, 2, d), (-d, k, B_HALF[d]), (d, 0))
                    near(head, ("x", k, d), (-d, k, B_PART))
                else:
                    arrive(head, ("x", k, 2, d), (2, k, B_HALF[d]))
            if step == 2:
                near(head, ("x", k), (2, k, B_PART))

    def on_y(head, distance, k):
        for j in (-1, 1) if distance == 1 else [distance]:
            for d in DIRS:
                if k < 4:
                    arrive(head, ("y", j, k, d), (j, -d * k, A_PART))
                    part = A_PART if k < 3 else A_HALF[d]
                    remote(head, ("y", j, k + 1, d), (j, -d * k, part), (0, d))
                    near(head, ("y", j, k, d), (j, -d * k, A_PART))
                else:
                    arrive(head, ("y", j, 4, d), (j, 4, A_HALF[d]))
            if k == 4:
                near(head, ("y", j, 4), (j, 4, A_PART))

    handlers = {"a": on_a, "b": on_b, "x": on_x, "y": on_y}

    def event(head, what):
        handlers[what[0]](head, *what[1:])

    def near_done(head):
        ref = bufs[head].at[1 - c]
        pltpu.make_async_remote_copy(
            src_ref=ref, dst_ref=ref, send_sem=near_send.at[0], recv_sem=near_recv.at[head],
            device_id=partner, device_id_type=MESH,
        ).wait_recv()

    def compute(head, iteration):
        buf, per = bufs[head], PER[head]
        ones_at = low if head == 0 else jnp.logical_not(low)
        one, out = (0, HDIM) if head == 0 else (HDIM, 0)
        units = [iteration * per + u for u in range(per)]

        def keys(t):
            return buf[tab[0, t], tab[1, t], tab[2, t], tab[3, t]]

        m, a = high[...], acc[...]
        scores, weights, scales = {}, {}, {}
        for step in range(per + 3):
            if step < per:
                t = units[step]
                scores[step] = lax.dot_general(
                    keys(t), qz[head, tab[4, t]], (((1,), (1,)), ((), ())), preferred_element_type=F32
                )
            u = step - 2
            if 0 <= u < per:
                s = scores.pop(u)
                m_prev = m + fresh[0, units[u]]
                m = jnp.maximum(m_prev, jnp.max(s, axis=0, keepdims=True))
                weights[u] = jnp.exp(s - m).astype(BF)
                scales[u] = jnp.exp(m_prev - m)
            u = step - 3
            if 0 <= u < per:
                kv = keys(units[u])
                side = jnp.where(ones_at, jnp.ones_like(kv), kv)
                a = a * scales.pop(u) + lax.dot_general(
                    side, weights.pop(u), (((0,), (0,)), ((), ())), preferred_element_type=F32
                )
                slots[units[u]] = (a[out : out + HDIM] * (1.0 / a[one : one + 1])).astype(BF)
        high[...] = m
        acc[...] = a

    chunk = FR // 4 * TOKF
    z_sent = []

    def ring_copy(ref, sems, k, d, device):
        return pltpu.make_async_remote_copy(
            src_ref=ref, dst_ref=ref, send_sem=sems[0].at[2 * (k - 1) + (d < 0)],
            recv_sem=sems[1].at[2 * (k - 1) + (d < 0)], device_id=device, device_id_type=MESH,
        )

    def z_copy(head, half, k, d, back):
        rows = pl.ds(half * chunk, chunk)
        if k == 4:
            rows = pl.ds(half * chunk + (d < 0) * (chunk // 2), chunk // 2)
        number = head * 2 + half
        ref = mzs[head].at[ring(z - d * (k - 1) - d * back, Z), rows, :]
        return ring_copy(ref, (z_send.at[number], z_recv.at[number]), k, d, zat(d))

    def w_copy(k, d, back):
        rows = pl.ds((d < 0) * HDIM, HDIM) if k == 4 else pl.ds(0, 2 * HDIM)
        ref = wbuf.at[ring(z - d * (k - 1) - d * back, Z), rows, :]
        return ring_copy(ref, (w_send, w_recv), k, d, zat(d))

    def w_start(k, d):
        w_copy(k, d, 0).start()
        z_sent.append(lambda: w_copy(k, d, 0))

    def on_w(k):
        for d in DIRS:
            w_copy(k, d, 1).wait_recv()
            if k < 4:
                w_start(k + 1, d)

    def z_start(head, half, k, d):
        z_copy(head, half, k, d, 0).start()
        z_sent.append(lambda: z_copy(head, half, k, d, 0))

    def merge(head):
        for half in (0, 1):
            for f in (2 * half, 2 * half + 1):
                both = jnp.concatenate([slots[tab[5, f]], slots[tab[5, f + FR // 2]]], axis=0)
                mzs[head][z, pl.ds(f * TOKF, TOKF), :] = both.T
            for d in DIRS:
                z_start(head, half, 1, d)
        for half in (0, 1):
            project(head, half, z, begin=head == 0)

    def on_z(head, k):
        for half in (0, 1):
            for d in DIRS:
                z_copy(head, half, k, d, 1).wait_recv()
                if k < 4:
                    z_start(head, half, k + 1, d)
            for d in DIRS if k < 4 else (1,):
                project(head, half, ring(z - d * k, Z))

    def project(head, half, source, begin=False):
        w = wbuf[source, pl.ds(head * HDIM, HDIM), pl.ds(pl.multiple_of(z * 128, 128), 128)]
        nil = jnp.zeros_like(w)
        wide = jnp.concatenate(
            [jnp.concatenate([w, nil], axis=1), jnp.concatenate([nil, w], axis=1)], axis=0
        )
        rows = pl.ds(half * chunk, chunk)
        term = jnp.dot(mzs[head][source, rows, :], wide, preferred_element_type=F32)
        total[rows, :] = term if begin else total[rows, :] + term

    def own(head, axis):
        (own_x if axis == "x" else own_y)(head)

    handlers.update(
        own=own, merge=merge, z=on_z, w=lambda head, k: on_w(k)
    )

    wbuf[z] = w_ref[...]
    own_x(0)
    own_y(0)
    for d in DIRS:
        w_start(1, d)
    prepare(1)
    high[...] = jnp.zeros_like(high)
    acc[...] = jnp.zeros_like(acc)
    for entry in AHEAD:
        event(*entry)
    near_done(0)

    @pl.loop(0, UNITS // PER[0])
    def _(iteration):
        for number, entry in BESIDE:
            pl.when(iteration == number)(lambda entry=entry: event(*entry))
        compute(0, iteration)

    for entry in AFTER:
        event(*entry)
    near_done(1)

    @pl.loop(0, UNITS // PER[1])
    def _(iteration):
        compute(1, iteration)

    merge(1)
    for k in (1, 2, 3, 4):
        on_z(1, k)
    for f in range(FR):
        side = f // (FR // 2)
        rows = (f % (FR // 2)) * TOKF
        o_ref[pl.ds(f * TOKF, TOKF), :] = total[
            pl.ds(rows, TOKF), pl.ds(side * 128, 128)
        ].astype(BF)
    for name, spec in sent.items():
        link_copy(1, name, spec, partner).wait_send()
    for name, spec in near_sent.items():
        near_copy(1, name, spec).wait_send()
    for copy in z_sent:
        copy().wait_send()


def body(query_states, key_states, value_states, pair_list, out_weight):
    me = lax.axis_index("frames")
    fresh, tab = tables(pair_list, me)
    vmem = pl.BlockSpec(memory_space=pltpu.VMEM)
    smem = pl.BlockSpec(memory_space=pltpu.SMEM)
    return pl.pallas_call(
        kernel,
        out_shape=jax.ShapeDtypeStruct((ROWS, 128), BF),
        in_specs=[smem, smem, vmem, vmem, vmem, vmem],
        out_specs=vmem,
        scratch_shapes=[
            pltpu.VMEM((2, X, Y, FR, TOKF, 128), BF),
            pltpu.VMEM((2, X, Y, FR, TOKF, 128), BF),
            pltpu.VMEM((UNITS, HDIM, TOKF), BF),
            pltpu.VMEM((2, FR, TOKF, 128), BF),
            pltpu.VMEM((Z, FR // 2 * TOKF, 128), BF),
            pltpu.VMEM((Z, FR // 2 * TOKF, 128), BF),
            pltpu.VMEM((Z, 128, 1024), BF),
            pltpu.VMEM((FR // 2 * TOKF, 256), F32),
            pltpu.VMEM((1, TOKF), F32),
            pltpu.VMEM((128, TOKF), F32),
            pltpu.SemaphoreType.DMA((76,)),
            pltpu.SemaphoreType.DMA((63,)),
            pltpu.SemaphoreType.DMA((2,)),
            pltpu.SemaphoreType.DMA((2, 76)),
            pltpu.SemaphoreType.DMA((8,)),
            pltpu.SemaphoreType.DMA((8,)),
            pltpu.SemaphoreType.DMA((4, 8)),
            pltpu.SemaphoreType.DMA((4, 8)),
        ],
        compiler_params=pltpu.CompilerParams(
            collective_id=0, has_side_effects=True, vmem_limit_bytes=63 * 2**20
        ),
        name="scene_attention",
    )(tab, fresh, query_states, key_states, value_states, out_weight)


def solution(mesh):
    placed = (
        P("frames", "heads"),
        P("frames", "heads"),
        P("frames", "heads"),
        P(),
        P("heads", None),
    )
    return jax.shard_map(
        body, mesh=mesh, in_specs=placed, out_specs=P("frames", "heads"), check_vma=False
    )
```

time: 283 us -> 193 us (0.68)
  the two profiles are of different devices: /device:TPU:80 before, /device:TPU:24 now
where the time goes in v1:
time: 193 us
  Pallas kernels  188 us (97%)
  local copies, waits for them, and re-layouts  3.45 us (2%)
    pallas_call x1, Pallas kernels, body(): pl.pallas_call(kernel, out_shape=jax.ShapeDtypeStruct((ROWS, 128), BF), i...  188 us

profile of v1, /device:TPU:24, one launch (start us, length us, event | category | flops | bytes accessed | tf_op | source)
XLA Modules:
  0.0 193.0 jit_solution(2282409971685961881)
XLA Ops:
  0.0 0.9 slice_reduce_fusion
  0.9 0.1 reshape_squeeze.7
  1.0 0.1 reshape_squeeze.6
  1.1 0.1 select_reduce_fusion.4
  1.2 0.1 pad_add_fusion
  1.3 0.1 pad_add_fusion.1
  1.4 0.2 convert_reduce_fusion.1
  1.6 0.2 select_reduce_fusion
  1.8 0.6 compare_select_fusion.5
  2.5 0.6 stack.5.tab
  3.1 188.2 %scene_attention.1 = bf16[1536,128]{1,0:T(8,128)(2,1)} custom-call(s32[6,136]{1,0:T(8,128)} %stack.5.tab, f32[1,136]{1,0:T(1,128)} %bitcast.10, bf16[1536,128]{1,0:T(8,128)(2,1)} %q_ref.1, bf16[1536,128]{1,0:T(8,128)(2,1)} %k_ref.1, bf16[1536,128]{1,0:T(8,128)(2,1)} %v_ref.1, bf16[128,1024]{1,0:T(8,128)(2,1)} %w_ref.1), custom_call_target="tpu_custom_call" | custom-call | tf_op jit(solution)/shard_map/scene_attention/pallas_call | solution.py:464
  191.3 1.8 copy.7
  (10 shorter events, 0.1 us)

commit v2 on v1

v2 whole, which is shorter than its diff:
```python
import jax
import jax.numpy as jnp
from jax import lax
from jax.experimental import pallas as pl
from jax.experimental.pallas import tpu as pltpu
from jax.sharding import PartitionSpec as P

MESH = pl.DeviceIdType.MESH
BF = jnp.bfloat16
F32 = jnp.float32
TOKF, HDIM = 192, 64
X, Y, Z = 4, 8, 8
FR = 8
ROWS = FR * TOKF
DEVICES = 2 * X * Y
RA = 48
RB = TOKF - RA
HALVES = {1: (0, FR // 2), -1: (FR // 2, FR // 2)}
ALL = (0, FR)
OFFSETS = (0, -1, 1, -2, 2, -3, 3, 4)
UNITS = 136
PER = (8, 17)
COPIES = 148
DIRS = (1, -1)
AHEAD = (
    (0, ("a", 1)),
    (0, ("r", 0)),
    (0, ("w", 1)),
    (0, ("b", 1)),
    (0, ("a", 2)),
    (0, ("y", 0, 1)),
    (0, ("y", 1, 1)),
    (0, ("r", 1)),
    (0, ("w", 2)),
    (0, ("b", 2)),
    (0, ("y", 2, 1)),
    (0, ("w", 3)),
    (0, ("y", 0, 2)),
    (0, ("r", 2)),
    (0, ("w", 4)),
    (0, ("y", 1, 2)),
    (0, ("b", 3)),
    (0, ("y", 2, 2)),
    (0, ("y", 0, 3)),
    (0, ("r", 3)),
    (0, ("y", 1, 3)),
    (0, ("b", 4)),
    (0, ("y", 2, 3)),
    (0, ("y", 0, 4)),
    (0, ("y", 1, 4)),
    (0, ("r", 4)),
    (1, ("own", "x")),
    (1, ("own", "y")),
    (0, ("y", 2, 4)),
)
BESIDE = (
    (1, (1, ("a", 1))),
    (2, (1, ("r", 0))),
    (3, (1, ("b", 1))),
    (4, (1, ("y", 0, 1))),
    (6, (1, ("a", 2))),
    (8, (1, ("y", 1, 1))),
    (10, (1, ("r", 1))),
    (14, (1, ("b", 2))),
    (16, (1, ("y", 0, 2))),
)
AFTER = (
    (1, ("y", 2, 1)),
    (0, ("merge",)),
    (1, ("r", 2)),
    (1, ("y", 1, 2)),
    (0, ("z", 1)),
    (1, ("b", 3)),
    (1, ("y", 0, 3)),
    (1, ("y", 2, 2)),
    (0, ("z", 2)),
    (1, ("r", 3)),
    (1, ("y", 1, 3)),
    (1, ("b", 4)),
    (1, ("y", 0, 4)),
    (0, ("z", 3)),
    (1, ("y", 2, 3)),
    (1, ("y", 1, 4)),
    (1, ("r", 4)),
    (1, ("y", 2, 4)),
    (0, ("z", 4)),
)


def tables(pair_list, me):
    first = pair_list[:, 0].reshape(64, 64)
    second = pair_list[:, 1].reshape(64, 64)
    hit = (second // FR)[:, None, :] == jnp.arange(64, dtype=jnp.int32)[None, :, None]
    both = jnp.sum(jnp.where(hit, (first * 512 + second)[:, None, :], 0), axis=2)
    mine = lax.dynamic_index_in_dim(both, me, 0, keepdims=False)
    back = lax.dynamic_index_in_dim(both, me, 1, keepdims=False)
    here = jnp.arange(FR, dtype=jnp.int32)
    frame = jnp.concatenate([here, mine // 512 - me * FR, back % 512 - me * FR])
    other = jnp.concatenate([here + me * FR, mine % 512, back // 512])
    number = jnp.arange(UNITS, dtype=jnp.int32)
    ahead = (frame[None, :] < frame[:, None]) | (
        (frame[None, :] == frame[:, None]) & (number[None, :] < number[:, None])
    )
    place = jnp.sum(ahead.astype(jnp.int32), axis=1)
    kind = (number >= FR).astype(jnp.int32) + (number >= FR + 64).astype(jnp.int32)
    packed = (kind * 512 + other) * FR + frame
    packed = jnp.sum(jnp.where(place[None, :] == number[:, None], packed[None, :], 0), axis=1)
    frame_at, other_at, kind_at = packed % FR, (packed // FR) % 512, packed // (FR * 512)
    fresh = jnp.where(kind_at > 0, 0.0, -jnp.inf).astype(F32)
    last = jnp.sum((frame[None, :] <= number[:, None]).astype(jnp.int32), axis=1) - 1
    device = other_at // FR
    place_of = (device % 2) * (X * Y) + device // 2
    own_slot = 2 * DEVICES + frame_at
    slot = jnp.where(kind_at > 0, 2 * place_of + kind_at - 1, own_slot)
    asked = jnp.stack([both % FR, (both // 512) % FR])
    return asked, fresh[None, :], jnp.stack(
        [place_of, other_at % FR, slot // 2, slot % 2, frame_at, last, last, last]
    )


def kernel(
    asked, tab, fresh, q_ref, k_ref, v_ref, w_ref, o_ref,
    buf0, buf1, *rest,
):
    raws = (rest[:8], rest[8:16])
    (
        rec0, rec1, pack0, pack1, relay0, relay1, slots, qz, mz0, mz1, wbuf, total, high, acc, send_sem, near_recv, rec_recv, recv_sem, w_send, w_recv, z_send, z_recv,
    ) = rest[16:]
    bufs, mzs = (buf0, buf1), (mz0, mz1)
    recs, packs, relays = (rec0, rec1), (pack0, pack1), (relay0, relay1)
    me = lax.axis_index("frames")
    z = lax.axis_index("heads")
    x, y, c = me // (2 * Y), (me // 2) % Y, me % 2

    def ring(value, size):
        return lax.rem(value + 4 * size, size)

    def at(dx, dy, dc=0):
        return (ring(x + dx, X) * (2 * Y) + ring(y + dy, Y) * 2 + (c + dc) % 2, z)

    def slot_of(dx, dy):
        return c * (X * Y) + ring(x + dx, X) * Y + ring(y + dy, Y)

    partner = (x * (2 * Y) + y * 2 + (1 - c), z)

    def zat(dz):
        return (me, ring(z + dz, Z))

    barrier = pltpu.get_barrier_semaphore()
    peers = [at(1, 0), at(-1, 0), at(1, 0, 1), at(-1, 0, 1), at(0, 1), at(0, -1), partner] + [zat(1), zat(-1)]
    for peer in peers:
        pl.semaphore_signal(barrier, inc=1, device_id=peer, device_id_type=MESH)

    lane = lax.broadcasted_iota(jnp.int32, (TOKF, 128), 1)
    low = lane < HDIM

    def prepare(head):
        for f in range(FR):
            rows = pl.ds(f * TOKF, TOKF)
            turned = pltpu.roll(v_ref[rows, :], HDIM, 1)
            keyed = k_ref[rows, :]
            block = jnp.where(low, keyed, turned) if head == 0 else jnp.where(low, turned, keyed)
            bufs[head][slot_of(0, 0), f] = block[:RA]
            raws[head][0][f] = block[RA:]
            recs[head][DEVICES + f // 2, f % 2] = block[RA:]
            query = q_ref[rows, :] * jnp.asarray(0.125, BF)
            nil = jnp.zeros_like(query)
            qz[head, f] = jnp.where(low, query, nil) if head == 0 else jnp.where(low, nil, query)

    prepare(0)
    pl.semaphore_wait(barrier, len(peers))

    names = {}

    def sem_of(name):
        return names.setdefault(name, len(names))

    sent = {}
    def ends(head, name):
        kind = name[0]
        if kind in ("a", "y", "near"):
            dx, dy, part = {"a": a_spec, "y": y_spec, "near": near_spec}[kind](*name[1:])
            ref = bufs[head].at[slot_of(dx, dy), pl.ds(part[0], part[1])]
            return ref, ref
        if kind == "b":
            k, d = name[1:]
            there = -d * k if k < 4 else 4
            part = HALVES[d] if k == 4 else ALL
            frames = pl.ds(part[0], part[1])
            return (
                raws[head][OFFSETS.index(-d * (k - 1))].at[frames],
                raws[head][OFFSETS.index(there)].at[frames],
            )
        if kind == "p":
            number, to = name[1:]
            if to >= 5:
                return packs[head].at[number, to], relays[head].at[number, to - 5]
            return packs[head].at[number, to], recs[head].at[slot_of(0, OFFSETS[number])]
        number, d = name[1:]
        return (
            relays[head].at[number, 0 if d > 0 else 1],
            recs[head].at[slot_of(-d, OFFSETS[number])],
        )

    def a_spec(step, d):
        return (0, 0, ALL) if step == 1 else (-d, 0, HALVES[d])

    def y_spec(j, k, d):
        return (j, -d * (k - 1), ALL if k < 4 else HALVES[d])

    def near_spec(dx, dy):
        return (dx, dy, ALL)

    def hop(name):
        kind = name[0]
        if kind == "a":
            return (name[2], 0, 0)
        if kind in ("b", "y"):
            return (0, name[-1], 0)
        if kind == "near":
            return (0, 0, 1)
        if kind == "p":
            return ((0, 0, 1), (1, 0, 0), (1, 0, 1), (-1, 0, 0), (-1, 0, 1), (1, 0, 0), (-1, 0, 0))[name[2]]
        return (name[2], 0, 0 if name[2] > 0 else 1)

    def link_copy(head, name):
        number = sem_of(name)
        kind = name[0]
        if kind == "near":
            arrived = near_recv.at[head]
        elif kind == "r" or kind == "p" and name[2] < 5:
            arrived = rec_recv.at[head]
        else:
            arrived = recv_sem.at[head, number]
        source, target = ends(head, name)
        return pltpu.make_async_remote_copy(
            src_ref=source, dst_ref=target, send_sem=send_sem.at[number], recv_sem=arrived,
            device_id=at(*hop(name)), device_id_type=MESH,
        )

    def remote(head, *name):
        if head == 1:
            link_copy(0, name).wait_send()
        link_copy(head, name).start()
        sent[name] = True

    def arrive(head, ref, *name):
        pltpu.make_async_remote_copy(
            src_ref=ref, dst_ref=ref, send_sem=send_sem.at[sem_of(name)],
            recv_sem=recv_sem.at[head, sem_of(name)], device_id=partner, device_id_type=MESH,
        ).wait_recv()

    def a_block(head, dx, dy, part=ALL):
        return bufs[head].at[slot_of(dx, dy), pl.ds(part[0], part[1])]

    def device_at(dx, dy, dc):
        return at(dx, dy, dc)[0]

    def pack(head, number):
        source = device_at(0, OFFSETS[number], 0)
        targets = ((0, 0), (0, 1), (1, 0), (1, 1), (-1, 0), (-1, 1), (2, 0), (2, 1))
        for to, (dx, dc) in enumerate(targets):
            target = device_at(dx, 0, dc)
            wanted = (asked[0, target, source], asked[1, source, target])
            for j in (0, 1):
                rows = raws[head][number][wanted[j]]
                if to == 0:
                    recs[head][slot_of(0, OFFSETS[number]), j] = rows
                else:
                    packs[head][number, to - 1, j] = rows
        for to in (5, 6, 1, 2, 3, 4, 0):
            remote(head, "p", number, to)

    def on_r(head, distance):
        for number, offset in enumerate(OFFSETS):
            if abs(offset) == distance:
                for d in DIRS:
                    arrive(head, relays[head].at[number, 0 if d > 0 else 1], "p", number, 5 if d > 0 else 6)
                    remote(head, "r", number, d)

    def start_y(head, j):
        for d in DIRS:
            remote(head, "y", j, 1, d)

    def own_x(head):
        for d in DIRS:
            remote(head, "a", 1, d)
        pack(head, 0)
        remote(head, "near", 0, 0)

    def own_y(head):
        for d in DIRS:
            remote(head, "b", 1, d)
        start_y(head, 0)

    def on_a(head, step):
        if step == 1:
            for d in DIRS:
                arrive(head, a_block(head, -d, 0), "a", 1, d)
                remote(head, "a", 2, d)
                start_y(head, -d)
                remote(head, "near", -d, 0)
        else:
            for d in DIRS:
                arrive(head, a_block(head, 2, 0, HALVES[d]), "a", 2, d)
            start_y(head, 2)
            remote(head, "near", 2, 0)

    def on_b(head, k):
        for d in DIRS:
            number = OFFSETS.index(-d * k if k < 4 else 4)
            part = HALVES[d] if k == 4 else ALL
            arrive(head, raws[head][number].at[pl.ds(part[0], part[1])], "b", k, d)
            if k < 4:
                remote(head, "b", k + 1, d)
        for number, offset in enumerate(OFFSETS):
            if abs(offset) == k:
                pack(head, number)

    def on_y(head, distance, k):
        for j in (-1, 1) if distance == 1 else [distance]:
            for d in DIRS:
                if k < 4:
                    arrive(head, a_block(head, j, -d * k), "y", j, k, d)
                    remote(head, "y", j, k + 1, d)
                    remote(head, "near", j, -d * k)
                else:
                    arrive(head, a_block(head, j, 4, HALVES[d]), "y", j, 4, d)
            if k == 4:
                remote(head, "near", j, 4)

    handlers = {"a": on_a, "b": on_b, "r": on_r, "y": on_y}

    def event(head, what):
        handlers[what[0]](head, *what[1:])

    def near_done(head):
        for ref, arrived in (
            (bufs[head].at[pl.ds(0, DEVICES // 2)], near_recv),
            (recs[head].at[pl.ds(0, DEVICES - Y)], rec_recv),
        ):
            pltpu.make_async_remote_copy(
                src_ref=ref, dst_ref=ref, send_sem=send_sem.at[0], recv_sem=arrived.at[head],
                device_id=partner, device_id_type=MESH,
            ).wait_recv()

    def compute(head, iteration):
        per = PER[head]
        ones_at = low if head == 0 else jnp.logical_not(low)
        one, out = (0, HDIM) if head == 0 else (HDIM, 0)
        units = [iteration * per + u for u in range(per)]

        def keys(t):
            return jnp.concatenate(
                [bufs[head][tab[0, t], tab[1, t]], recs[head][tab[2, t], tab[3, t]]], axis=0
            )

        m, a = high[...], acc[...]
        scores, weights, scales = {}, {}, {}
        for step in range(per + 3):
            if step < per:
                t = units[step]
                scores[step] = lax.dot_general(
                    keys(t), qz[head, tab[4, t]], (((1,), (1,)), ((), ())), preferred_element_type=F32
                )
            u = step - 2
            if 0 <= u < per:
                s = scores.pop(u)
                m_prev = m + fresh[0, units[u]]
                m = jnp.maximum(m_prev, jnp.max(s, axis=0, keepdims=True))
                weights[u] = jnp.exp(s - m).astype(BF)
                scales[u] = jnp.exp(m_prev - m)
            u = step - 3
            if 0 <= u < per:
                kv = keys(units[u])
                side = jnp.where(ones_at, jnp.ones_like(kv), kv)
                a = a * scales.pop(u) + lax.dot_general(
                    side, weights.pop(u), (((0,), (0,)), ((), ())), preferred_element_type=F32
                )
                slots[units[u]] = (a[out : out + HDIM] * (1.0 / a[one : one + 1])).astype(BF)
        high[...] = m
        acc[...] = a

    chunk = FR // 4 * TOKF
    z_sent = []

    def ring_copy(ref, sems, k, d, device):
        return pltpu.make_async_remote_copy(
            src_ref=ref, dst_ref=ref, send_sem=sems[0].at[2 * (k - 1) + (d < 0)],
            recv_sem=sems[1].at[2 * (k - 1) + (d < 0)], device_id=device, device_id_type=MESH,
        )

    def z_copy(head, half, k, d, back):
        rows = pl.ds(half * chunk, chunk)
        if k == 4:
            rows = pl.ds(half * chunk + (d < 0) * (chunk // 2), chunk // 2)
        number = head * 2 + half
        ref = mzs[head].at[ring(z - d * (k - 1) - d * back, Z), rows, :]
        return ring_copy(ref, (z_send.at[number], z_recv.at[number]), k, d, zat(d))

    def w_copy(k, d, back):
        rows = pl.ds((d < 0) * HDIM, HDIM) if k == 4 else pl.ds(0, 2 * HDIM)
        ref = wbuf.at[ring(z - d * (k - 1) - d * back, Z), rows, :]
        return ring_copy(ref, (w_send, w_recv), k, d, zat(d))

    def w_start(k, d):
        w_copy(k, d, 0).start()
        z_sent.append(lambda: w_copy(k, d, 0))

    def on_w(k):
        for d in DIRS:
            w_copy(k, d, 1).wait_recv()
            if k < 4:
                w_start(k + 1, d)

    def z_start(head, half, k, d):
        z_copy(head, half, k, d, 0).start()
        z_sent.append(lambda: z_copy(head, half, k, d, 0))

    def merge(head):
        for half in (0, 1):
            for f in (2 * half, 2 * half + 1):
                both = jnp.concatenate([slots[tab[5, f]], slots[tab[5, f + FR // 2]]], axis=0)
                mzs[head][z, pl.ds(f * TOKF, TOKF), :] = both.T
            for d in DIRS:
                z_start(head, half, 1, d)
        for half in (0, 1):
            project(head, half, z, begin=head == 0)

    def on_z(head, k):
        for half in (0, 1):
            for d in DIRS:
                z_copy(head, half, k, d, 1).wait_recv()
                if k < 4:
                    z_start(head, half, k + 1, d)
            for d in DIRS if k < 4 else (1,):
                project(head, half, ring(z - d * k, Z))

    def project(head, half, source, begin=False):
        w = wbuf[source, pl.ds(head * HDIM, HDIM), pl.ds(pl.multiple_of(z * 128, 128), 128)]
        nil = jnp.zeros_like(w)
        wide = jnp.concatenate(
            [jnp.concatenate([w, nil], axis=1), jnp.concatenate([nil, w], axis=1)], axis=0
        )
        rows = pl.ds(half * chunk, chunk)
        term = jnp.dot(mzs[head][source, rows, :], wide, preferred_element_type=F32)
        total[rows, :] = term if begin else total[rows, :] + term

    def own(head, axis):
        (own_x if axis == "x" else own_y)(head)

    handlers.update(
        own=own, merge=merge, z=on_z, w=lambda head, k: on_w(k)
    )

    wbuf[z] = w_ref[...]
    own_x(0)
    own_y(0)
    for d in DIRS:
        w_start(1, d)
    prepare(1)
    high[...] = jnp.zeros_like(high)
    acc[...] = jnp.zeros_like(acc)
    for entry in AHEAD:
        event(*entry)
    near_done(0)

    @pl.loop(0, UNITS // PER[0])
    def _(iteration):
        for number, entry in BESIDE:
            pl.when(iteration == number)(lambda entry=entry: event(*entry))
        compute(0, iteration)

    for entry in AFTER:
        event(*entry)
    near_done(1)

    @pl.loop(0, UNITS // PER[1])
    def _(iteration):
        compute(1, iteration)

    merge(1)
    for k in (1, 2, 3, 4):
        on_z(1, k)
    for f in range(FR):
        side = f // (FR // 2)
        rows = (f % (FR // 2)) * TOKF
        o_ref[pl.ds(f * TOKF, TOKF), :] = total[
            pl.ds(rows, TOKF), pl.ds(side * 128, 128)
        ].astype(BF)
    for name in sent:
        link_copy(1, name).wait_send()
    for copy in z_sent:
        copy().wait_send()


def body(query_states, key_states, value_states, pair_list, out_weight):
    me = lax.axis_index("frames")
    asked, fresh, tab = tables(pair_list, me)
    vmem = pl.BlockSpec(memory_space=pltpu.VMEM)
    smem = pl.BlockSpec(memory_space=pltpu.SMEM)
    return pl.pallas_call(
        kernel,
        out_shape=jax.ShapeDtypeStruct((ROWS, 128), BF),
        in_specs=[smem, smem, smem, vmem, vmem, vmem, vmem],
        out_specs=vmem,
        scratch_shapes=[
            pltpu.VMEM((DEVICES, FR, RA, 128), BF),
            pltpu.VMEM((DEVICES, FR, RA, 128), BF),
            *[pltpu.VMEM((FR, RB, 128), BF) for _ in range(16)],
            pltpu.VMEM((DEVICES + FR // 2, 2, RB, 128), BF),
            pltpu.VMEM((DEVICES + FR // 2, 2, RB, 128), BF),
            pltpu.VMEM((8, 7, 2, RB, 128), BF),
            pltpu.VMEM((8, 7, 2, RB, 128), BF),
            pltpu.VMEM((8, 2, 2, RB, 128), BF),
            pltpu.VMEM((8, 2, 2, RB, 128), BF),
            pltpu.VMEM((UNITS, HDIM, TOKF), BF),
            pltpu.VMEM((2, FR, TOKF, 128), BF),
            pltpu.VMEM((Z, FR // 2 * TOKF, 128), BF),
            pltpu.VMEM((Z, FR // 2 * TOKF, 128), BF),
            pltpu.VMEM((Z, 128, 1024), BF),
            pltpu.VMEM((FR // 2 * TOKF, 256), F32),
            pltpu.VMEM((1, TOKF), F32),
            pltpu.VMEM((128, TOKF), F32),
            pltpu.SemaphoreType.DMA((COPIES,)),
            pltpu.SemaphoreType.DMA((2,)),
            pltpu.SemaphoreType.DMA((2,)),
            pltpu.SemaphoreType.DMA((2, COPIES)),
            pltpu.SemaphoreType.DMA((8,)),
            pltpu.SemaphoreType.DMA((8,)),
            pltpu.SemaphoreType.DMA((4, 8)),
            pltpu.SemaphoreType.DMA((4, 8)),
        ],
        compiler_params=pltpu.CompilerParams(
            collective_id=0, has_side_effects=True, vmem_limit_bytes=63 * 2**20
        ),
        name="scene_attention",
    )(asked, tab, fresh, query_states, key_states, value_states, out_weight)


def solution(mesh):
    placed = (
        P("frames", "heads"),
        P("frames", "heads"),
        P("frames", "heads"),
        P(),
        P("heads", None),
    )
    return jax.shard_map(
        body, mesh=mesh, in_specs=placed, out_specs=P("frames", "heads"), check_vma=False
    )
```

time: 193 us -> 171 us (0.89)
  the two profiles are of different devices: /device:TPU:24 before, /device:TPU:2 now
where the time goes in v2:
time: 171 us; the launch traced here: 170 us
  Pallas kernels  164 us (96%)
  other arithmetic  3.87 us (2%)
  local copies, waits for them, and re-layouts  2.71 us (2%)
    pallas_call x1, Pallas kernels, body(): pl.pallas_call(kernel, out_shape=jax.ShapeDtypeStruct((ROWS, 128), BF), i...  164 us

profile of v2, /device:TPU:2, one launch (start us, length us, event | category | flops | bytes accessed | tf_op | source)
XLA Modules:
  0.0 170.5 jit_solution(10436306163737390202)
XLA Ops:
  0.0 0.9 slice_reduce_fusion
  0.9 0.1 reshape_squeeze.4
  1.0 0.1 mul.75
  1.1 1.2 select_reduce_fusion
  2.3 0.2 dynamic-slice_reduce_fusion
  2.5 0.1 pad_add_fusion.2
  2.6 0.2 convert_reduce_fusion
  2.8 0.1 select_reduce_fusion.1
  2.9 0.6 compare_select_fusion.11
  3.6 0.6 stack.5.tab
  4.2 0.6 pad_add_fusion.asked
  4.9 163.8 %scene_attention.1 = bf16[1536,128]{1,0:T(8,128)(2,1)} custom-call(s32[2,64,64]{2,1,0:T(8,128)} %pad_add_fusion.asked, s32[8,136]{1,0:T(8,128)} %stack.5.tab, f32[1,136]{1,0:T(1,128)} %get-tuple-element.9.fresh, bf16[1536,128]{1,0:T(8,128)(2,1)} %q_ref.1, bf16[1536,128]{1,0:T(8,128)(2,1)} %k_ref.1, bf16[1536,128]{1,0:T(8,128)(2,1)} %v_ref.1, ...), custom_call_target="tpu_custom_call" | custom-call | tf_op jit(solution)/shard_map/scene_attention/pallas_call | solution.py:502
  168.7 1.8 %copy.7 = bf16[1536,128]{1,0:T(8,128)(2,1)} copy(bf16[1536,128]{1,0:T(8,128)(2,1)} %scene_attention.1) | data formatting | bytes 786432
  (12 shorter events, 0.2 us)

commit v3 on v2

--- a/solution.py
+++ b/solution.py
@@ -19,6 +19,7 @@
 ALL = (0, FR)
 OFFSETS = (0, -1, 1, -2, 2, -3, 3, 4)
 UNITS = 136
+FRESH = -1e30
 PER = (8, 17)
 COPIES = 148
 DIRS = (1, -1)
@@ -37,8 +38,8 @@
     (0, ("w", 3)),
     (0, ("y", 0, 2)),
     (0, ("r", 2)),
+    (0, ("y", 1, 2)),
     (0, ("w", 4)),
-    (0, ("y", 1, 2)),
     (0, ("b", 3)),
     (0, ("y", 2, 2)),
     (0, ("y", 0, 3)),
@@ -47,51 +48,50 @@
     (0, ("b", 4)),
     (0, ("y", 2, 3)),
     (0, ("y", 0, 4)),
+    (1, ("own", "y")),
     (0, ("y", 1, 4)),
     (0, ("r", 4)),
     (1, ("own", "x")),
-    (1, ("own", "y")),
     (0, ("y", 2, 4)),
 )
 BESIDE = (
+    (1, (1, ("b", 1))),
     (1, (1, ("a", 1))),
     (2, (1, ("r", 0))),
-    (3, (1, ("b", 1))),
-    (4, (1, ("y", 0, 1))),
-    (6, (1, ("a", 2))),
-    (8, (1, ("y", 1, 1))),
-    (10, (1, ("r", 1))),
-    (14, (1, ("b", 2))),
+    (2, (1, ("y", 0, 1))),
+    (9, (1, ("r", 1))),
+    (10, (1, ("b", 2))),
+    (14, (1, ("y", 1, 1))),
+    (15, (1, ("a", 2))),
     (16, (1, ("y", 0, 2))),
 )
 AFTER = (
+    (0, ("merge",)),
+    (1, ("b", 3)),
+    (1, ("r", 2)),
+    (0, ("z", 1)),
+    (1, ("y", 1, 2)),
     (1, ("y", 2, 1)),
-    (0, ("merge",)),
-    (1, ("r", 2)),
-    (1, ("y", 1, 2)),
-    (0, ("z", 1)),
-    (1, ("b", 3)),
     (1, ("y", 0, 3)),
+    (1, ("r", 3)),
+    (1, ("b", 4)),
+    (0, ("z", 2)),
+    (1, ("y", 1, 3)),
     (1, ("y", 2, 2)),
-    (0, ("z", 2)),
-    (1, ("r", 3)),
-    (1, ("y", 1, 3)),
-    (1, ("b", 4)),
     (1, ("y", 0, 4)),
     (0, ("z", 3)),
+    (1, ("y", 1, 4)),
     (1, ("y", 2, 3)),
-    (1, ("y", 1, 4)),
     (1, ("r", 4)),
+    (0, ("z", 4)),
     (1, ("y", 2, 4)),
-    (0, ("z", 4)),
 )
 
 
 def tables(pair_list, me):
-    first = pair_list[:, 0].reshape(64, 64)
-    second = pair_list[:, 1].reshape(64, 64)
-    hit = (second // FR)[:, None, :] == jnp.arange(64, dtype=jnp.int32)[None, :, None]
-    both = jnp.sum(jnp.where(hit, (first * 512 + second)[:, None, :], 0), axis=2)
+    coded = jnp.sum(pair_list * jnp.array([512, 1], jnp.int32), axis=1).reshape(64, 64)
+    hit = ((coded % 512) // FR)[:, None, :] == jnp.arange(64, dtype=jnp.int32)[None, :, None]
+    both = jnp.sum(jnp.where(hit, coded[:, None, :], 0), axis=2)
     mine = lax.dynamic_index_in_dim(both, me, 0, keepdims=False)
     back = lax.dynamic_index_in_dim(both, me, 1, keepdims=False)
     here = jnp.arange(FR, dtype=jnp.int32)
@@ -102,24 +102,19 @@
         (frame[None, :] == frame[:, None]) & (number[None, :] < number[:, None])
     )
     place = jnp.sum(ahead.astype(jnp.int32), axis=1)
-    kind = (number >= FR).astype(jnp.int32) + (number >= FR + 64).astype(jnp.int32)
-    packed = (kind * 512 + other) * FR + frame
-    packed = jnp.sum(jnp.where(place[None, :] == number[:, None], packed[None, :], 0), axis=1)
-    frame_at, other_at, kind_at = packed % FR, (packed // FR) % 512, packed // (FR * 512)
-    fresh = jnp.where(kind_at > 0, 0.0, -jnp.inf).astype(F32)
-    last = jnp.sum((frame[None, :] <= number[:, None]).astype(jnp.int32), axis=1) - 1
-    device = other_at // FR
+    device = other // FR
     place_of = (device % 2) * (X * Y) + device // 2
-    own_slot = 2 * DEVICES + frame_at
-    slot = jnp.where(kind_at > 0, 2 * place_of + kind_at - 1, own_slot)
-    asked = jnp.stack([both % FR, (both // 512) % FR])
-    return asked, fresh[None, :], jnp.stack(
-        [place_of, other_at % FR, slot // 2, slot % 2, frame_at, last, last, last]
-    )
+    behind = (number >= FR + 64).astype(jnp.int32)
+    own = number < FR
+    slot = jnp.where(own, 2 * DEVICES + frame, 2 * place_of + behind)
+    unit = (((own.astype(jnp.int32) * 256 + slot) * 64 + place_of) * FR + other % FR) * FR + frame
+    unit = jnp.sum(jnp.where(place[None, :] == number[:, None], unit[None, :], 0), axis=1)
+    last = jnp.sum((frame[None, :] <= here[:, None]).astype(jnp.int32), axis=1) - 1
+    return both, unit, last
 
 
 def kernel(
-    asked, tab, fresh, q_ref, k_ref, v_ref, w_ref, o_ref,
+    both, unit, last, q_ref, k_ref, v_ref, w_ref, o_ref,
     buf0, buf1, *rest,
 ):
     raws = (rest[:8], rest[8:16])
@@ -261,7 +256,7 @@
         targets = ((0, 0), (0, 1), (1, 0), (1, 1), (-1, 0), (-1, 1), (2, 0), (2, 1))
         for to, (dx, dc) in enumerate(targets):
             target = device_at(dx, 0, dc)
-            wanted = (asked[0, target, source], asked[1, source, target])
+            wanted = (both[target, source] & 7, (both[source, target] >> 9) & 7)
             for j in (0, 1):
                 rows = raws[head][number][wanted[j]]
                 if to == 0:
@@ -352,7 +347,7 @@
 
         def keys(t):
             return jnp.concatenate(
-                [bufs[head][tab[0, t], tab[1, t]], recs[head][tab[2, t], tab[3, t]]], axis=0
+                [bufs[head][(unit[t] >> 6) & 63, (unit[t] >> 3) & 7], recs[head][(unit[t] >> 13) & 127, (unit[t] >> 12) & 1]], axis=0
             )
 
         m, a = high[...], acc[...]
@@ -361,12 +356,12 @@
             if step < per:
                 t = units[step]
                 scores[step] = lax.dot_general(
-                    keys(t), qz[head, tab[4, t]], (((1,), (1,)), ((), ())), preferred_element_type=F32
+                    keys(t), qz[head, unit[t] & 7], (((1,), (1,)), ((), ())), preferred_element_type=F32
                 )
             u = step - 2
             if 0 <= u < per:
                 s = scores.pop(u)
-                m_prev = m + fresh[0, units[u]]
+                m_prev = m + (unit[units[u]] >> 20).astype(F32) * FRESH
                 m = jnp.maximum(m_prev, jnp.max(s, axis=0, keepdims=True))
                 weights[u] = jnp.exp(s - m).astype(BF)
                 scales[u] = jnp.exp(m_prev - m)
@@ -420,7 +415,7 @@
     def merge(head):
         for half in (0, 1):
             for f in (2 * half, 2 * half + 1):
-                both = jnp.concatenate([slots[tab[5, f]], slots[tab[5, f + FR // 2]]], axis=0)
+                both = jnp.concatenate([slots[last[f]], slots[last[f + FR // 2]]], axis=0)
                 mzs[head][z, pl.ds(f * TOKF, TOKF), :] = both.T
             for d in DIRS:
                 z_start(head, half, 1, d)
@@ -496,7 +491,7 @@
 
 def body(query_states, key_states, value_states, pair_list, out_weight):
     me = lax.axis_index("frames")
-    asked, fresh, tab = tables(pair_list, me)
+    both, unit, last = tables(pair_list, me)
     vmem = pl.BlockSpec(memory_space=pltpu.VMEM)
     smem = pl.BlockSpec(memory_space=pltpu.SMEM)
     return pl.pallas_call(
@@ -535,7 +530,7 @@
             collective_id=0, has_side_effects=True, vmem_limit_bytes=63 * 2**20
         ),
         name="scene_attention",
-    )(asked, tab, fresh, query_states, key_states, value_states, out_weight)
+    )(both, unit, last, query_states, key_states, value_states, out_weight)
 
 
 def solution(mesh):

time: 171 us -> 168 us (0.982)
  Pallas kernels: 164 us -> 162 us
    pallas_call x1, Pallas kernels: 164 us -> 162 us  [body(): pl.pallas_call(kernel, out_shape=jax.ShapeDtypeStruct((ROWS, 128), BF), i...]
where the time goes in v3:
time: 168 us; the launch traced here: 167 us
  Pallas kernels  162 us (96%)
  other arithmetic  3.76 us (2%)
  local copies, waits for them, and re-layouts  2.02 us (1%)
    pallas_call x1, Pallas kernels, body(): pl.pallas_call(kernel, out_shape=jax.ShapeDtypeStruct((ROWS, 128), BF), i...  162 us

profile of v3, /device:TPU:2, one launch (start us, length us, event | category | flops | bytes accessed | tf_op | source)
XLA Modules:
  0.0 167.4 jit_solution(3718747288614062778)
XLA Ops:
  0.0 0.9 multiply_reduce_fusion
  0.9 0.1 reshape.250
  1.0 1.2 select_reduce_fusion.both
  2.2 0.0 copy-start
  2.2 0.2 dynamic-slice_reduce_fusion
  2.4 0.1 pad_add_fusion.1
  2.5 0.1 convert_reduce_fusion.1
  2.6 0.2 convert_reduce_fusion
  2.8 0.7 select_reduce_fusion.1.unit
  3.5 0.5 broadcast_add_fusion.last
  4.1 0.0 copy-done
  4.1 161.6 %scene_attention.1 = bf16[1536,128]{1,0:T(8,128)(2,1)} custom-call(s32[64,64]{1,0:T(8,128)} %copy-done, s32[136]{0:T(256)} %select_reduce_fusion.1.unit, s32[8]{0:T(128)} %broadcast_add_fusion.last, bf16[1536,128]{1,0:T(8,128)(2,1)} %q_ref.1, bf16[1536,128]{1,0:T(8,128)(2,1)} %k_ref.1, bf16[1536,128]{1,0:T(8,128)(2,1)} %v_ref.1, bf16[128,1024]{1,0:T(8,128)(2,1)} %w_ref.1), custom_call_target="tpu_custom_call" | custom-call | tf_op jit(solution)/shard_map/scene_attention/pallas_call | solution.py:497
  165.6 1.8 %copy.8 = bf16[1536,128]{1,0:T(8,128)(2,1)} copy(bf16[1536,128]{1,0:T(8,128)(2,1)} %scene_attention.1) | data formatting | bytes 786432
  (6 shorter events, 0.1 us)
Async XLA Ops:
  2.2 1.9 %copy-start = (s32[64,64]{1,0:T(8,128)}, s32[64,64]{1,0:T(8,128)S(1)}, u32[]{:S(2)}) copy-start(s32[64,64]{1,0:T(8,128)S(1)} %select_reduce_fusion.both) | copy-start | bytes 49156

commit v4 on v3

--- a/solution.py
+++ b/solution.py
@@ -20,7 +20,7 @@
 OFFSETS = (0, -1, 1, -2, 2, -3, 3, 4)
 UNITS = 136
 FRESH = -1e30
-PER = (8, 17)
+PER = (8, 34)
 COPIES = 148
 DIRS = (1, -1)
 AHEAD = (
@@ -352,20 +352,20 @@
 
         m, a = high[...], acc[...]
         scores, weights, scales = {}, {}, {}
-        for step in range(per + 3):
+        for step in range(per + 5):
             if step < per:
                 t = units[step]
                 scores[step] = lax.dot_general(
                     keys(t), qz[head, unit[t] & 7], (((1,), (1,)), ((), ())), preferred_element_type=F32
                 )
-            u = step - 2
+            u = step - 4
             if 0 <= u < per:
                 s = scores.pop(u)
                 m_prev = m + (unit[units[u]] >> 20).astype(F32) * FRESH
                 m = jnp.maximum(m_prev, jnp.max(s, axis=0, keepdims=True))
                 weights[u] = jnp.exp(s - m).astype(BF)
                 scales[u] = jnp.exp(m_prev - m)
-            u = step - 3
+            u = step - 5
             if 0 <= u < per:
                 kv = keys(units[u])
                 side = jnp.where(ones_at, jnp.ones_like(kv), kv)
@@ -428,6 +428,7 @@
                 z_copy(head, half, k, d, 1).wait_recv()
                 if k < 4:
                     z_start(head, half, k + 1, d)
+        for half in (0, 1):
             for d in DIRS if k < 4 else (1,):
                 project(head, half, ring(z - d * k, Z))
 

time: 168 us -> 164 us (0.976)
  Pallas kernels: 162 us -> 158 us
    pallas_call x1, Pallas kernels: 162 us -> 158 us  [body(): pl.pallas_call(kernel, out_shape=jax.ShapeDtypeStruct((ROWS, 128), BF), i...]
where the time goes in v4:
time: 164 us
  Pallas kernels  158 us (96%)
  other arithmetic  3.76 us (2%)
  local copies, waits for them, and re-layouts  2.02 us (1%)
    pallas_call x1, Pallas kernels, body(): pl.pallas_call(kernel, out_shape=jax.ShapeDtypeStruct((ROWS, 128), BF), i...  158 us

profile of v4, /device:TPU:2, one launch (start us, length us, event | category | flops | bytes accessed | tf_op | source)
XLA Modules:
  0.0 163.9 jit_solution(3538069139050389043)
XLA Ops:
  0.0 0.9 multiply_reduce_fusion
  0.9 0.1 reshape.250
  1.0 1.2 select_reduce_fusion.both
  2.2 0.0 copy-start
  2.2 0.2 dynamic-slice_reduce_fusion
  2.4 0.1 pad_add_fusion.1
  2.5 0.1 convert_reduce_fusion.1
  2.6 0.2 convert_reduce_fusion
  2.8 0.7 select_reduce_fusion.1.unit
  3.5 0.5 broadcast_add_fusion.last
  4.1 0.0 copy-done
  4.1 158.1 %scene_attention.1 = bf16[1536,128]{1,0:T(8,128)(2,1)} custom-call(s32[64,64]{1,0:T(8,128)} %copy-done, s32[136]{0:T(256)} %select_reduce_fusion.1.unit, s32[8]{0:T(128)} %broadcast_add_fusion.last, bf16[1536,128]{1,0:T(8,128)(2,1)} %q_ref.1, bf16[1536,128]{1,0:T(8,128)(2,1)} %k_ref.1, bf16[1536,128]{1,0:T(8,128)(2,1)} %v_ref.1, bf16[128,1024]{1,0:T(8,128)(2,1)} %w_ref.1), custom_call_target="tpu_custom_call" | custom-call | tf_op jit(solution)/shard_map/scene_attention/pallas_call | solution.py:498
  162.2 1.8 %copy.8 = bf16[1536,128]{1,0:T(8,128)(2,1)} copy(bf16[1536,128]{1,0:T(8,128)(2,1)} %scene_attention.1) | data formatting | bytes 786432
  (6 shorter events, 0.1 us)
Async XLA Ops:
  2.2 1.9 %copy-start = (s32[64,64]{1,0:T(8,128)}, s32[64,64]{1,0:T(8,128)S(1)}, u32[]{:S(2)}) copy-start(s32[64,64]{1,0:T(8,128)S(1)} %select_reduce_fusion.both) | copy-start | bytes 49156

commit v5 on v4

--- a/solution.py
+++ b/solution.py
@@ -376,7 +376,8 @@
         high[...] = m
         acc[...] = a
 
-    chunk = FR // 4 * TOKF
+    chunk = TOKF
+    parts = range(FR // 2)
     z_sent = []
 
     def ring_copy(ref, sems, k, d, device):
@@ -385,11 +386,11 @@
             recv_sem=sems[1].at[2 * (k - 1) + (d < 0)], device_id=device, device_id_type=MESH,
         )
 
-    def z_copy(head, half, k, d, back):
-        rows = pl.ds(half * chunk, chunk)
+    def z_copy(head, part, k, d, back):
+        rows = pl.ds(part * chunk, chunk)
         if k == 4:
-            rows = pl.ds(half * chunk + (d < 0) * (chunk // 2), chunk // 2)
-        number = head * 2 + half
+            rows = pl.ds(part * chunk + (d < 0) * (chunk // 2), chunk // 2)
+        number = head * (FR // 2) + part
         ref = mzs[head].at[ring(z - d * (k - 1) - d * back, Z), rows, :]
         return ring_copy(ref, (z_send.at[number], z_recv.at[number]), k, d, zat(d))
 
@@ -408,37 +409,37 @@
             if k < 4:
                 w_start(k + 1, d)
 
-    def z_start(head, half, k, d):
-        z_copy(head, half, k, d, 0).start()
-        z_sent.append(lambda: z_copy(head, half, k, d, 0))
+    def z_start(head, part, k, d):
+        z_copy(head, part, k, d, 0).start()
+        z_sent.append(lambda: z_copy(head, part, k, d, 0))
 
     def merge(head):
-        for half in (0, 1):
-            for f in (2 * half, 2 * half + 1):
+        for part in parts:
+            for f in (part,):
                 both = jnp.concatenate([slots[last[f]], slots[last[f + FR // 2]]], axis=0)
                 mzs[head][z, pl.ds(f * TOKF, TOKF), :] = both.T
             for d in DIRS:
-                z_start(head, half, 1, d)
-        for half in (0, 1):
-            project(head, half, z, begin=head == 0)
+                z_start(head, part, 1, d)
+        for part in parts:
+            project(head, part, z, begin=head == 0)
 
     def on_z(head, k):
-        for half in (0, 1):
+        for part in parts:
             for d in DIRS:
-                z_copy(head, half, k, d, 1).wait_recv()
+                z_copy(head, part, k, d, 1).wait_recv()
                 if k < 4:
-                    z_start(head, half, k + 1, d)
-        for half in (0, 1):
+                    z_start(head, part, k + 1, d)
+        for part in parts:
             for d in DIRS if k < 4 else (1,):
-                project(head, half, ring(z - d * k, Z))
-
-    def project(head, half, source, begin=False):
+                project(head, part, ring(z - d * k, Z))
+
+    def project(head, part, source, begin=False):
         w = wbuf[source, pl.ds(head * HDIM, HDIM), pl.ds(pl.multiple_of(z * 128, 128), 128)]
         nil = jnp.zeros_like(w)
         wide = jnp.concatenate(
             [jnp.concatenate([w, nil], axis=1), jnp.concatenate([nil, w], axis=1)], axis=0
         )
-        rows = pl.ds(half * chunk, chunk)
+        rows = pl.ds(part * chunk, chunk)
         term = jnp.dot(mzs[head][source, rows, :], wide, preferred_element_type=F32)
         total[rows, :] = term if begin else total[rows, :] + term
 
@@ -524,8 +525,8 @@
             pltpu.SemaphoreType.DMA((2, COPIES)),
             pltpu.SemaphoreType.DMA((8,)),
             pltpu.SemaphoreType.DMA((8,)),
-            pltpu.SemaphoreType.DMA((4, 8)),
-            pltpu.SemaphoreType.DMA((4, 8)),
+            pltpu.SemaphoreType.DMA((FR, 8)),
+            pltpu.SemaphoreType.DMA((FR, 8)),
         ],
         compiler_params=pltpu.CompilerParams(
             collective_id=0, has_side_effects=True, vmem_limit_bytes=63 * 2**20

time: 164 us -> 164 us (level)
  the two profiles are of different devices: /device:TPU:2 before, /device:TPU:24 now
where the time goes in v5:
time: 164 us
  Pallas kernels  158 us (96%)
  other arithmetic  3.76 us (2%)
  local copies, waits for them, and re-layouts  2.02 us (1%)
    pallas_call x1, Pallas kernels, body(): pl.pallas_call(kernel, out_shape=jax.ShapeDtypeStruct((ROWS, 128), BF), i...  158 us

profile of v5, /device:TPU:24, one launch (start us, length us, event | category | flops | bytes accessed | tf_op | source)
XLA Modules:
  0.0 163.8 jit_solution(9394925414466091528)
XLA Ops:
  0.0 0.9 multiply_reduce_fusion
  0.9 0.1 reshape.250
  1.0 1.2 select_reduce_fusion.both
  2.2 0.0 copy-start
  2.2 0.2 dynamic-slice_reduce_fusion
  2.4 0.1 pad_add_fusion.1
  2.5 0.1 convert_reduce_fusion.1
  2.6 0.2 convert_reduce_fusion
  2.8 0.7 select_reduce_fusion.1.unit
  3.5 0.5 broadcast_add_fusion.last
  4.1 0.0 copy-done
  4.1 158.0 %scene_attention.1 = bf16[1536,128]{1,0:T(8,128)(2,1)} custom-call(s32[64,64]{1,0:T(8,128)} %copy-done, s32[136]{0:T(256)} %select_reduce_fusion.1.unit, s32[8]{0:T(128)} %broadcast_add_fusion.last, bf16[1536,128]{1,0:T(8,128)(2,1)} %q_ref.1, bf16[1536,128]{1,0:T(8,128)(2,1)} %k_ref.1, bf16[1536,128]{1,0:T(8,128)(2,1)} %v_ref.1, bf16[128,1024]{1,0:T(8,128)(2,1)} %w_ref.1), custom_call_target="tpu_custom_call" | custom-call | tf_op jit(solution)/shard_map/scene_attention/pallas_call | solution.py:499
  162.1 1.8 %copy.8 = bf16[1536,128]{1,0:T(8,128)(2,1)} copy(bf16[1536,128]{1,0:T(8,128)(2,1)} %scene_attention.1) | data formatting | bytes 786432
  (6 shorter events, 0.1 us)
Async XLA Ops:
  2.2 1.9 %copy-start = (s32[64,64]{1,0:T(8,128)}, s32[64,64]{1,0:T(8,128)S(1)}, u32[]{:S(2)}) copy-start(s32[64,64]{1,0:T(8,128)S(1)} %select_reduce_fusion.both) | copy-start | bytes 49156
